TPU v7x, 32 devices: a whole 2x2x4 slice. The times are simulated.
32 devices in a mesh: parts: 2 (over x), xline: 16 (over z, y, core).
Axes of the slice: x: 2, y: 2, z: 4, core: 2. Of those that a mesh axis runs over, the one named last changes fastest.
Arguments:
- gathers: bfloat16 [4, 96, 96, 256], P('parts', 'xline'), parts along dimension 0, may hold values from -6 to 6
- time_steps: float32 [2], replicated, may hold values from 0.3 to 0.8
- radon_op: bfloat16 [32, 2, 96, 96], P('xline'), may hold values from -0.4375 to 0.4375
Outputs:
- conditioned: bfloat16 [4, 96, 96, 256], P('parts', 'xline'), parts along dimension 0
There are 2 independent parts, one for each index of `parts`. A program takes and returns all parts, laid end to end along the dimension named above; an argument that names none is the same for every part. Nothing has to cross between parts.
All inputs are finite; a program needn't handle non-finite values.
Results may differ from a plain program's by a relative error of at most 0.0072.
Values may be sent and summed in bfloat16 or wider, within the bound.
A program may use at most 128 MiB of HBM per device.

v0:
```python
import math

import jax
import jax.numpy as jnp
from jax import lax
from jax.sharding import PartitionSpec as P


def diff_depth(field):
    padded = jnp.pad(field, ((0, 0), (0, 0), (0, 0), (1, 1)))
    return 0.5 * (padded[..., 2:] - padded[..., :-2])


def box_depth(field):
    padded = jnp.pad(field, ((0, 0), (0, 0), (0, 0), (1, 1)))
    return (padded[..., :-2] + padded[..., 1:-1] + padded[..., 2:]) / 3.0


def diff_cross(field):
    return 0.5 * (field[:, 2:] - field[:, :-2])


def box_cross(field):
    return (field[:, :-2] + field[:, 1:-1] + field[:, 2:]) / 3.0


def diffuse(extended, tau_value, columns, total):
    inside = ((columns >= 0) & (columns < total)).astype(jnp.float32)[None, :, None, None]
    grad_cross = diff_cross(extended) * inside[:, 1:-1]
    grad_depth = diff_depth(extended[:, 1:-1]) * inside[:, 1:-1]
    tensor_xx = box_cross(box_depth(grad_cross * grad_cross)) * inside[:, 2:-2]
    tensor_xz = box_cross(box_depth(grad_cross * grad_depth)) * inside[:, 2:-2]
    tensor_zz = box_cross(box_depth(grad_depth * grad_depth)) * inside[:, 2:-2]
    norm_term = 1.0 + tensor_xx + tensor_zz
    inner_x = grad_cross[:, 1:-1]
    inner_z = grad_depth[:, 1:-1]
    flux_cross = inner_x - (tensor_xx * inner_x + tensor_xz * inner_z) / norm_term
    flux_depth = inner_z - (tensor_xz * inner_x + tensor_zz * inner_z) / norm_term
    change = diff_cross(flux_cross) + diff_depth(flux_depth[:, 1:-1])
    return (extended[:, 3:-3] + tau_value * change) * inside[:, 3:-3]


def forward_table(depth, bins):
    zeds = jnp.arange(depth, dtype=jnp.int32)[:, None]
    freqs = jnp.arange(bins, dtype=jnp.int32)[None, :]
    phase = (zeds * freqs % depth).astype(jnp.float32) * (2.0 * math.pi / depth)
    return jnp.concatenate([jnp.cos(phase), -jnp.sin(phase)], axis=1).astype(jnp.bfloat16)


def inverse_table(depth, bins):
    freqs = jnp.arange(bins, dtype=jnp.int32)[:, None]
    zeds = jnp.arange(depth, dtype=jnp.int32)[None, :]
    phase = (zeds * freqs % depth).astype(jnp.float32) * (2.0 * math.pi / depth)
    weight = jnp.where(freqs == 0, 1.0, 2.0).astype(jnp.float32) / depth
    return jnp.concatenate([weight * jnp.cos(phase), -weight * jnp.sin(phase)], axis=0).astype(
        jnp.bfloat16
    )


def complex_mats(operators):
    real_row = jnp.stack([operators[:, 0], -operators[:, 1]], axis=1)
    imag_row = jnp.stack([operators[:, 1], operators[:, 0]], axis=1)
    return jnp.stack([real_row, imag_row], axis=1)


def per_device(gathers, time_steps, radon_op):
    inlines, lines, offsets, depth = gathers.shape
    devices = lax.axis_size("xline")
    total = lines * devices
    bins = radon_op.shape[0] * devices
    steps_count = time_steps.shape[0]
    traces = jnp.transpose(gathers, (0, 2, 1, 3)).reshape(inlines * offsets, lines, depth)
    local_rows = lax.all_to_all(traces, "xline", split_axis=0, concat_axis=1, tiled=True)
    pair_rows = local_rows.shape[0]
    field = local_rows.astype(jnp.float32).reshape(pair_rows, total, 1, depth)
    columns = jnp.arange(-3, total + 3, dtype=jnp.int32)
    for number in range(steps_count):
        extended = jnp.pad(field, ((0, 0), (3, 3), (0, 0), (0, 0)))
        field = diffuse(extended, time_steps[number], columns, total)
    smooth = field.astype(jnp.bfloat16)
    spectrum = jnp.dot(
        smooth.reshape(-1, depth), forward_table(depth, bins), preferred_element_type=jnp.float32
    )
    spectrum = spectrum.astype(jnp.bfloat16).reshape(pair_rows, total, 2, bins)
    by_bins = lax.all_to_all(spectrum, "xline", split_axis=3, concat_axis=0, tiled=True)
    by_bins = by_bins.reshape(inlines, offsets, total, 2, radon_op.shape[0])
    mats = complex_mats(radon_op)
    done = jnp.einsum("ioxrf,fqrpo->ipxqf", by_bins, mats, preferred_element_type=jnp.float32)
    done = done.astype(jnp.bfloat16)
    back = lax.all_to_all(done, "xline", split_axis=2, concat_axis=4, tiled=True)
    filtered = jnp.transpose(back, (0, 2, 1, 3, 4))
    result = jnp.dot(
        filtered.reshape(-1, 2 * bins),
        inverse_table(depth, bins),
        preferred_element_type=jnp.float32,
    )
    return result.astype(jnp.bfloat16).reshape(inlines, lines, offsets, depth)


def solution(mesh):
    return jax.shard_map(
        per_device,
        mesh=mesh,
        in_specs=(P("parts", "xline", None, None), P(), P("xline", None, None, None)),
        out_specs=P("parts", "xline", None, None),
        check_vma=False,
    )
```

profile of v0, /device:TPU:0, one launch (start us, length us, event | category | flops | bytes accessed | tf_op | source)
XLA Modules:
  0.0 80.5 jit_solution(15486866586063491887)
XLA Ops:
  0.0 1.1 %copy.34 = bf16[2,6,96,256]{3,2,0,1:T(8,128)(2,1)S(1)} copy(bf16[2,6,96,256]{3,2,1,0:T(8,128)(2,1)} %param.3) | data formatting | bytes 1179648 | tf_op args[0]
  1.1 1.2 %copy.35 = bf16[192,6,256]{2,1,0:T(8,128)(2,1)} copy(bf16[192,6,256]{2,0,1:T(8,128)(2,1)S(1)} %bitcast.56) | data formatting | bytes 1179648 | tf_op jit(solution)/shard_map/reshape | solution.py:72
  2.3 7.4 %all-to-all-start = ((bf16[192,6,256]{2,1,0:T(8,128)(2,1)}), bf16[192,6,256]{2,1,0:T(8,128)(2,1)S(1)}, u32[]{:S(2)}, u32[]{:S(2)}) async-start(bf16[192,6,256]{2,1,0:T(8,128)(2,1)} %copy.35), calls=%async_computation | async-start | bytes 1572864 | tf_op jit(solution)/shard_map/all_to_all | solution.py:73
  9.8 0.6 fusion.81
  11.6 0.1 negate_convert_fusion
  12.0 16.4 %all-to-all-done = bf16[192,6,256]{2,1,0:T(8,128)(2,1)S(1)} async-done(((bf16[192,6,256]{2,1,0:T(8,128)(2,1)}), bf16[192,6,256]{2,1,0:T(8,128)(2,1)S(1)}, u32[]{:S(2)}, u32[]{:S(2)}) %all-to-all-start) | async-done | bytes 589856 | tf_op jit(solution)/shard_map/all_to_all | solution.py:73
  28.6 0.1 reshape.86
  28.7 0.7 copy.37
  29.4 0.2 reshape.85
  29.7 0.8 fusion.79
  30.5 0.2 mul.293
  30.7 0.2 mul.304
  30.9 0.7 fusion.10
  31.6 1.4 %fusion.2 = (f32[12,100,1,256]{3,1,0,2:T(8,128)S(1)}, f32[12,100,1,256]{3,1,0,2:T(8,128)S(1)}) fusion(f32[12,100,1,256]{3,1,0,2:T(8,128)S(1)} %mul.293, f32[12,100,1,256]{3,1,0,2:T(8,128)S(1)} %get-tuple-element.16), kind=kLoop, calls=%fused_computation.24 | loop fusion | flops 1843200 | bytes 4915200 | tf_op jit(solution)/shard_map/div | solution.py:16
  33.0 2.9 %divide_subtract_fusion.1 = (f32[12,98,1,256]{3,1,0,2:T(8,128)S(1)}, f32[12,98,1,256]{3,1,0,2:T(8,128)}, f32[12,98,1,256]{3,1,0,2:T(8,128)S(1)}, f32[12,98,1,256...) fusion(f32[12,100,1,256]{3,1,0,2:T(8,128)S(1)} %get-tuple-element.18, ...), kind=kLoop, calls=%fused_computation.65 | loop fusion | flops 4816896 | bytes 20472200 | tf_op jit(solution)/shard_map/sub | solution.py:37
  35.8 0.2 add_add_fusion.1
  36.0 1.1 %copy-done.2 = f32[12,98,1,256]{3,1,0,2:T(8,128)S(1)} copy-done((f32[12,98,1,256]{3,1,0,2:T(8,128)S(1)}, f32[12,98,1,256]{3,1,0,2:T(8,128)}, u32[]{:S(2)}) %copy-start.2) | copy-done | bytes 1204248
  37.1 0.4 copy-done.3
  37.5 0.4 copy-done.4
  37.9 0.7 fusion.41
  38.6 0.7 fusion.32
  39.5 0.8 fusion.74
  40.3 0.2 mul.317
  40.4 0.7 fusion.13
  41.2 0.2 mul.324
  41.3 0.7 fusion.21
  42.1 0.7 fusion.18
  42.8 3.0 %divide_subtract_fusion = (f32[12,98,1,256]{3,1,0,2:T(8,128)S(1)}, f32[12,98,1,256]{3,1,0,2:T(8,128)S(1)}, f32[12,98,1,256]{3,1,0,2:T(8,128)S(1)}, f32[12,98,1,2...) fusion(f32[12,100,1,256]{3,1,0,2:T(8,128)S(1)} %get-tuple-element.11, ...), kind=kLoop, calls=%fused_computation.62 | loop fusion | flops 4816896 | bytes 20472200 | tf_op jit(solution)/shard_map/sub | solution.py:37
  45.8 0.2 add_add_fusion
  46.0 1.1 %copy-done = f32[12,98,1,256]{3,1,0,2:T(8,128)S(1)} copy-done((f32[12,98,1,256]{3,1,0,2:T(8,128)S(1)}, f32[12,98,1,256]{3,1,0,2:T(8,128)}, u32[]{:S(2)}) %copy-start) | copy-done | bytes 1204248
  47.1 0.4 copy-done.1
  47.5 0.7 fusion.39
  48.3 0.7 fusion.38
  49.0 0.3 convolution_convert_fusion.1
  49.3 0.3 reshape.81
  49.6 0.9 %copy.38 = bf16[12,96,2,32]{1,2,0,3:T(2,128)(2,1)} copy(bf16[12,96,2,32]{1,0,3,2:T(8,128)(2,1)S(1)} %reshape.81) | data formatting | bytes 294912 | tf_op jit(solution)/shard_map/reshape | solution.py:84
  50.5 5.5 %all-to-all-start.1 = ((bf16[12,96,2,32]{1,2,0,3:T(2,128)(2,1)}), bf16[12,96,2,32]{1,2,0,3:T(2,128)(2,1)S(1)}, u32[]{:S(2)}, u32[]{:S(2)}) async-start(bf16[12,96,2,32]{1,2,0,3:T(2,128)(2,1)} %copy.38), calls=%async_computation.1 | async-start | bytes 393216 | tf_op jit(solution)/shard_map/all_to_all | solution.py:85
  56.1 8.9 %all-to-all-done.1 = bf16[12,96,2,32]{1,2,0,3:T(2,128)(2,1)S(1)} async-done(((bf16[12,96,2,32]{1,2,0,3:T(2,128)(2,1)}), bf16[12,96,2,32]{1,2,0,3:T(2,128)(2,1)S(1)}, u32[]{:S(2)}, u32[]{:S(2)}) %all-to-all-start.1) | async-done | bytes 147488 | tf_op jit(solution)/shard_map/all_to_all | solution.py:85
  65.0 0.2 copy.39
  65.2 0.3 fusion.44
  65.5 0.8 %copy.41 = bf16[2,96,96,2,2]{1,0,3,4,2:T(2,128)(2,1)} copy(bf16[2,96,96,2,2]{2,1,0,3,4:T(8,128)(2,1)S(1)} %fusion.44) | data formatting | bytes 294912 | tf_op jit(solution)/shard_map/convert_element_type | solution.py:89
  66.3 3.5 %all-to-all-start.2 = ((bf16[2,96,96,2,2]{1,0,3,4,2:T(2,128)(2,1)}), bf16[2,96,96,2,2]{1,0,3,4,2:T(2,128)(2,1)S(1)}, u32[]{:S(2)}, u32[]{:S(2)}) async-start(bf16[2,96,96,2,2]{1,0,3,4,2:T(2,128)(2,1)} %copy.41), calls=%async_computation.2 | async-start | bytes 393216 | tf_op jit(solution)/shard_map/all_to_all | solution.py:90
  69.8 0.1 multiply_convert_fusion
  70.0 8.8 %all-to-all-done.2 = bf16[2,96,96,2,2]{1,0,3,4,2:T(2,128)(2,1)S(1)} async-done(((bf16[2,96,96,2,2]{1,0,3,4,2:T(2,128)(2,1)}), bf16[2,96,96,2,2]{1,0,3,4,2:T(2,128)(2,1)S(1)}, u32[]{:S(2)}, u32[]{:S(2)}) %all-to-all-start.2) | async-done | bytes 147488 | tf_op jit(solution)/shard_map/all_to_all | solution.py:90
  78.8 0.2 copy.43
  79.0 0.1 copy.44
  79.1 0.2 reshape.83
  79.3 1.2 %convolution_convert_fusion = bf16[1152,256]{1,0:T(8,128)(2,1)} fusion(bf16[1152,64]{0,1:T(8,128)(2,1)S(1)} %reshape.83, bf16[32,256]{1,0:T(8,128)(2,1)S(1)} %get-tuple-element.34, bf16[32,256]{1,0:T(8,128)(2,1)S(1)} %get-tuple-element.35), kind=kOutput, calls=%fused_computation | convolution fusion | flops 38109184 | bytes 770048 | tf_op jit(solution)/shard_map/dot_general | solution.py:92
  (20 shorter events, 0.6 us)
Async XLA Ops:
  1.1 8.6 %copy-start.6 = (f32[2]{0:T(128)S(1)}, f32[2]{0:T(128)}, u32[]{:S(2)}) copy-start(f32[2]{0:T(128)} %param.4) | copy-start | bytes 28
  2.3 26.1 %all-to-all-start = ((bf16[192,6,256]{2,1,0:T(8,128)(2,1)}), bf16[192,6,256]{2,1,0:T(8,128)(2,1)S(1)}, u32[]{:S(2)}, u32[]{:S(2)}) async-start(bf16[192,6,256]{2,1,0:T(8,128)(2,1)} %copy.35), calls=%async_computation | async-start | bytes 1572864 | tf_op jit(solution)/shard_map/all_to_all | solution.py:73
  35.8 1.3 %copy-start.2 = (f32[12,98,1,256]{3,1,0,2:T(8,128)S(1)}, f32[12,98,1,256]{3,1,0,2:T(8,128)}, u32[]{:S(2)}) copy-start(f32[12,98,1,256]{3,1,0,2:T(8,128)} %get-tuple-element.13) | copy-start | bytes 3612676
  35.8 1.7 %copy-start.3 = (f32[12,98,1,256]{3,1,0,2:T(8,128)S(1)}, f32[12,98,1,256]{3,1,0,2:T(8,128)}, u32[]{:S(2)}) copy-start(f32[12,98,1,256]{3,1,0,2:T(8,128)} %get-tuple-element.21) | copy-start | bytes 3612676
  35.8 2.1 %copy-start.4 = (f32[12,98,1,256]{3,1,0,2:T(8,128)S(1)}, f32[12,98,1,256]{3,1,0,2:T(8,128)}, u32[]{:S(2)}) copy-start(f32[12,98,1,256]{3,1,0,2:T(8,128)} %get-tuple-element.22) | copy-start | bytes 3612676
  45.8 1.3 %copy-start = (f32[12,98,1,256]{3,1,0,2:T(8,128)S(1)}, f32[12,98,1,256]{3,1,0,2:T(8,128)}, u32[]{:S(2)}) copy-start(f32[12,98,1,256]{3,1,0,2:T(8,128)} %get-tuple-element.19) | copy-start | bytes 3612676
  45.8 1.7 %copy-start.1 = (f32[12,98,1,256]{3,1,0,2:T(8,128)S(1)}, f32[12,98,1,256]{3,1,0,2:T(8,128)}, u32[]{:S(2)}) copy-start(f32[12,98,1,256]{3,1,0,2:T(8,128)} %get-tuple-element.20) | copy-start | bytes 3612676
  49.0 7.0 %copy-start.5 = (bf16[2,2,96,96]{3,2,1,0:T(8,128)(2,1)S(1)}, bf16[2,2,96,96]{3,2,1,0:T(8,128)(2,1)}, u32[]{:S(2)}) copy-start(bf16[2,2,96,96]{3,2,1,0:T(8,128)(2,1)} %param.5) | copy-start | bytes 221188
  50.5 14.5 %all-to-all-start.1 = ((bf16[12,96,2,32]{1,2,0,3:T(2,128)(2,1)}), bf16[12,96,2,32]{1,2,0,3:T(2,128)(2,1)S(1)}, u32[]{:S(2)}, u32[]{:S(2)}) async-start(bf16[12,96,2,32]{1,2,0,3:T(2,128)(2,1)} %copy.38), calls=%async_computation.1 | async-start | bytes 393216 | tf_op jit(solution)/shard_map/all_to_all | solution.py:85
  66.3 12.5 %all-to-all-start.2 = ((bf16[2,96,96,2,2]{1,0,3,4,2:T(2,128)(2,1)}), bf16[2,96,96,2,2]{1,0,3,4,2:T(2,128)(2,1)S(1)}, u32[]{:S(2)}, u32[]{:S(2)}) async-start(bf16[2,96,96,2,2]{1,0,3,4,2:T(2,128)(2,1)} %copy.41), calls=%async_computation.2 | async-start | bytes 393216 | tf_op jit(solution)/shard_map/all_to_all | solution.py:90
where the time goes:
time: 81 us; the launch traced here: 80.5 us
  waiting for transfers between devices  34.1 us (42%)
  starting transfers between devices  16.4 us (20%)
  other arithmetic  16.3 us (20%)
  local copies, waits for them, and re-layouts  10.4 us (13%)
  matrix products  1.73 us (2%)
  between operations  1.56 us (2%)
    all_to_all x1, waiting for transfers between devices, per_device(): lax.all_to_all(traces, 'xline', split_axis=0, concat_axis=1, tiled=True)  16.4 us
    all_to_all x1, waiting for transfers between devices, per_device(): lax.all_to_all(spectrum, 'xline', split_axis=3, concat_axis=0, tiled=True)  8.9 us
    all_to_all x1, waiting for transfers between devices, per_device(): lax.all_to_all(done, 'xline', split_axis=2, concat_axis=4, tiled=True)  8.8 us
    all_to_all x1, starting transfers between devices, per_device(): lax.all_to_all(traces, 'xline', split_axis=0, concat_axis=1, tiled=True)  7.39 us
    sub x2, other arithmetic, diffuse(): inner_x - (tensor_xx * inner_x + tensor_xz * inner_z) / norm_term  5.89 us
    all_to_all x1, starting transfers between devices, per_device(): lax.all_to_all(spectrum, 'xline', split_axis=3, concat_axis=0, tiled=True)  5.47 us
    unnamed x15, local copies, waits for them, and re-layouts  4.54 us
    div x5, other arithmetic, box_depth(): return (padded[..., :-2] + padded[..., 1:-1] + padded[..., 2:]) / 3.0  4.28 us
  transfers between devices with their start and end apart: 3, of which 3 were waited for; matrix products, arithmetic and copies ran while one was open for 1% of the time, Pallas kernels for 0%

commit v1 on v0

v1 whole, which is shorter than its diff:
```python
import functools
import math

import jax
import jax.numpy as jnp
import ml_dtypes
import numpy as np
from jax import lax
from jax.experimental import pallas as pl
from jax.experimental.pallas import tpu as pltpu
from jax.sharding import PartitionSpec as P

ROWS = 16


def tables(depth, bins):
    phase = (np.arange(bins)[:, None] * np.arange(depth)[None, :] % depth) * (2.0 * math.pi / depth)
    weight = np.where(np.arange(bins) == 0, 1.0, 2.0)[:, None] / depth
    forward = np.stack([np.cos(phase), -np.sin(phase)], axis=1).reshape(2 * bins, depth)
    inverse = np.stack([weight * np.cos(phase), -weight * np.sin(phase)], axis=1).reshape(2 * bins, depth)
    diff = np.eye(depth, k=-1) - np.eye(depth, k=1)
    box = np.eye(depth, k=-1) + np.eye(depth) + np.eye(depth, k=1)
    return [a.astype(ml_dtypes.bfloat16) for a in (forward, inverse, diff, box)]


def dot(a, b):
    return jnp.dot(a, b, preferred_element_type=jnp.float32)


def dot_on(a, b, left, right):
    return lax.dot_general(a, b, (((left,), (right,)), ((), ())), preferred_element_type=jnp.float32)


def rows_of(line, count=1):
    return pl.ds(line * ROWS, count * ROWS)


def diffuse_step(width, load, keep, tau, last, scratch):
    field_s, half_s, gz_s, prod_s, tens_s, fx_s, fz_s, diff_ref, box_ref = scratch

    def grad(x):
        value = load(x + 1) - load(x - 1)
        return value if keep(x) is None else value * keep(x)

    gz_s[rows_of(0, width - 2), :] = dot(half_s[rows_of(1, width - 2), :], diff_ref[...])
    older = []
    for x in range(1, width - 1):
        gx, gz = grad(x), gz_s[rows_of(x - 1), :]
        older.append((gx * gx, gx * gz, gz * gz))
        if len(older) == 3:
            for number in range(3):
                total = older[0][number] + older[1][number] + older[2][number]
                prod_s[number, rows_of(x - 3), :] = total.astype(jnp.bfloat16)
            older.pop(0)
    for number in range(3):
        tens_s[number, rows_of(0, width - 4), :] = dot(
            prod_s[number, rows_of(0, width - 4), :], box_ref[...]
        )
    for x in range(2, width - 2):
        gx, gz = grad(x), gz_s[rows_of(x - 1), :]
        sxx, sxz, szz = (tens_s[number, rows_of(x - 2), :] for number in range(3))
        inverse = pl.reciprocal(36.0 + sxx + szz, approx=True)
        fx_s[rows_of(x - 2), :] = gx - (sxx * gx + sxz * gz) * inverse
        if 3 <= x < width - 3:
            fz_s[rows_of(x - 3), :] = (gz - (sxz * gx + szz * gz) * inverse).astype(jnp.bfloat16)
    gz_s[rows_of(0, width - 6), :] = dot(fz_s[rows_of(0, width - 6), :], diff_ref[...])
    for x in range(3, width - 3):
        change = fx_s[rows_of(x - 1), :] - fx_s[rows_of(x - 3), :] + gz_s[rows_of(x - 3), :]
        value = load(x) + tau * change
        if keep(x) is not None:
            value = value * keep(x)
        if last:
            yield x - 3, value
        else:
            field_s[rows_of(x - 3), :] = value
            half_s[rows_of(x - 3), :] = value.astype(jnp.bfloat16)


def kernel(
    tau_ref, own_ref, left_ref, right_ref, radon_ref, forward_ref, inverse_ref, diff_ref, box_ref,
    out_ref, first_s, field_s, half_s, gz_s, prod_s, tens_s, fx_s, fz_s, smooth_s, spec_s, filt_s,
):
    inlines, lines, offsets, depth = own_ref.shape
    halo = left_ref.shape[1]
    steps = halo // 3
    bins = radon_ref.shape[0]
    me = lax.axis_index("xline")
    keep_left = jnp.where(me > 0, 1.0, 0.0).astype(jnp.float32)
    keep_right = jnp.where(me < lax.axis_size("xline") - 1, 1.0, 0.0).astype(jnp.float32)
    scratch = (field_s, half_s, gz_s, prod_s, tens_s, fx_s, fz_s, diff_ref, box_ref)
    blocks = offsets // ROWS

    def chunk(number, carry):
        inline = number // blocks
        at = pl.ds(pl.multiple_of(number % blocks * ROWS, ROWS), ROWS)
        for x in range(halo):
            half_s[rows_of(x), :] = left_ref[inline, x, at, :]
            half_s[rows_of(halo + lines + x), :] = right_ref[inline, x, at, :]
        for x in range(lines):
            half_s[rows_of(halo + x), :] = own_ref[inline, x, at, :]
        first_s[...] = half_s[...].astype(jnp.float32)
        for step in range(steps):
            width = lines + 2 * (halo - 3 * step)
            border = halo - 3 * step

            def keep(x):
                if x < border:
                    return keep_left
                return keep_right if x >= border + lines else None

            source = first_s if step == 0 else field_s
            results = diffuse_step(
                width, lambda x: source[rows_of(x), :], keep, 0.25 * tau_ref[step],
                step == steps - 1, scratch,
            )
            for x, value in results:
                smooth_s[inline * lines + x, at, :] = value.astype(jnp.bfloat16)
        return carry

    lax.fori_loop(0, inlines * blocks, chunk, 0)

    count = inlines * lines
    slots = spec_s.shape[0] // (2 * bins)
    for n in range(count):
        value = dot_on(forward_ref[...], smooth_s[n], 1, 1)
        spec_s[pl.ds(n, 2 * bins, stride=slots), :] = value.astype(jnp.bfloat16).astype(jnp.float32)

    def one_bin(k, carry):
        base = pl.multiple_of(k * 2 * slots, 2 * slots)
        both = spec_s[pl.ds(base, 2 * slots), :].astype(jnp.bfloat16)
        by_real = dot_on(both, radon_ref[k, 0], 1, 1)
        by_imag = dot_on(both, radon_ref[k, 1], 1, 1)
        real = by_real[:slots] - by_imag[slots:]
        imag = by_imag[:slots] + by_real[slots:]
        filt_s[pl.ds(base, slots), :] = real.astype(jnp.bfloat16).astype(jnp.float32)
        filt_s[pl.ds(base + slots, slots), :] = imag.astype(jnp.bfloat16).astype(jnp.float32)
        return carry

    lax.fori_loop(0, bins, one_bin, 0, unroll=8)
    for n in range(count):
        value = filt_s[pl.ds(n, 2 * bins, stride=slots), :].astype(jnp.bfloat16)
        result = dot_on(value, inverse_ref[...], 0, 0)
        out_ref[n // lines, n % lines] = result.astype(jnp.bfloat16)


def per_device(gathers, time_steps, radon_op):
    inlines, lines, offsets, depth = gathers.shape
    devices = lax.axis_size("xline")
    bins = radon_op.shape[0] * devices
    halo = 3 * time_steps.shape[0]
    operators = lax.all_gather(radon_op, "xline", axis=0, tiled=True)
    left = lax.ppermute(
        gathers[:, lines - halo :], "xline", [(d, d + 1) for d in range(devices - 1)]
    )
    right = lax.ppermute(gathers[:, :halo], "xline", [(d + 1, d) for d in range(devices - 1)])
    width = lines + 2 * halo
    slots = -(-inlines * lines // 16) * 16
    vmem = pl.BlockSpec(memory_space=pltpu.VMEM)
    f32, bf16 = jnp.float32, jnp.bfloat16
    return pl.pallas_call(
        kernel,
        out_shape=jax.ShapeDtypeStruct(gathers.shape, bf16),
        in_specs=[pl.BlockSpec(memory_space=pltpu.SMEM)] + [vmem] * 8,
        out_specs=vmem,
        scratch_shapes=[
            pltpu.VMEM((width * ROWS, depth), f32),
            pltpu.VMEM((width * ROWS, depth), f32),
            pltpu.VMEM((width * ROWS, depth), bf16),
            pltpu.VMEM((width * ROWS, depth), f32),
            pltpu.VMEM((3, width * ROWS, depth), bf16),
            pltpu.VMEM((3, width * ROWS, depth), f32),
            pltpu.VMEM((width * ROWS, depth), f32),
            pltpu.VMEM((width * ROWS, depth), bf16),
            pltpu.VMEM((inlines * lines, offsets, depth), bf16),
            pltpu.VMEM((2 * bins * slots, offsets), f32),
            pltpu.VMEM((2 * bins * slots, offsets), f32),
        ],
        compiler_params=pltpu.CompilerParams(vmem_limit_bytes=48 * 2**20),
    )(time_steps, gathers, left, right, operators, *tables(depth, bins))


def solution(mesh):
    return jax.shard_map(
        per_device,
        mesh=mesh,
        in_specs=(P("parts", "xline", None, None), P(), P("xline", None, None, None)),
        out_specs=P("parts", "xline", None, None),
        check_vma=False,
    )
```

time: 81 us -> 82.1 us (1.014)
  other arithmetic: 16.3 us -> 0 us
  Pallas kernels: 0 us -> 14 us
  starting transfers between devices: 16.4 us -> 3.69 us
  between operations: 1.56 us -> 13.4 us
  waiting for transfers between devices: 34.1 us -> 44.1 us
  local copies, waits for them, and re-layouts: 10.4 us -> 6.45 us
  matrix products: 1.73 us -> 0 us
    all_gather x0 -> x1, waiting for transfers between devices: none -> 38.5 us  [per_device(): operators = lax.all_gather(radon_op, 'xline', axis=0, tiled=True)]
    all_to_all x3 -> x0, waiting for transfers between devices: 34.1 us -> none  [the longest x1 16.4 us: per_device(): lax.all_to_all(traces, 'xline', split_axis=0, concat_axis=1, tiled=True)]
    all_to_all x3 -> x0, starting transfers between devices: 16.4 us -> none  [the longest x1 7.39 us: per_device(): lax.all_to_all(traces, 'xline', split_axis=0, concat_axis=1, tiled=True)]
    pallas_call x0 -> x1, Pallas kernels: none -> 14 us  [per_device(): pl.pallas_call(kernel, out_shape=jax.ShapeDtypeStruct(gathers.shape, bf16...]
    sub x4 -> x0, other arithmetic: 7.38 us -> none  [the longest x2 5.89 us: diffuse(): inner_x - (tensor_xx * inner_x + tensor_xz * inner_z) / norm_term]
    ppermute x0 -> x2, waiting for transfers between devices: none -> 4.91 us  [the longest x1 4.42 us: per_device(): lax.ppermute(gathers[:, :halo], 'xline', [(d + 1, d) for d in range(devic...]
    div x6 -> x0, other arithmetic: 4.29 us -> none  [the longest x5 4.28 us: box_depth(): return (padded[..., :-2] + padded[..., 1:-1] + padded[..., 2:]) / 3.0]
    ppermute x0 -> x2, starting transfers between devices: none -> 3.69 us  [the longest x1 2.39 us: per_device(): lax.ppermute(gathers[:, lines - halo:], 'xline', [(d, d + 1) for d in ran...]
  transfers between devices with their start and end apart: 3 -> 3, of which waited for: 3 -> 3; matrix products, arithmetic and copies ran while one was open for 1% -> 0% of each run, Pallas kernels for 0% -> 0%
where the time goes in v1:
time: 82.1 us; the launch traced here: 81.7 us
  waiting for transfers between devices  44.1 us (54%)
  Pallas kernels  14 us (17%)
  between operations  13.4 us (16%)
  local copies, waits for them, and re-layouts  6.45 us (8%)
  starting transfers between devices  3.69 us (4%)
    all_gather x1, waiting for transfers between devices, per_device(): operators = lax.all_gather(radon_op, 'xline', axis=0, tiled=True)  38.5 us
    pallas_call x1, Pallas kernels, per_device(): pl.pallas_call(kernel, out_shape=jax.ShapeDtypeStruct(gathers.shape, bf16...  14 us
    unnamed x14, local copies, waits for them, and re-layouts  6.45 us
    ppermute x1, waiting for transfers between devices, per_device(): lax.ppermute(gathers[:, :halo], 'xline', [(d + 1, d) for d in range(devic...  4.42 us
    ppermute x1, starting transfers between devices, per_device(): lax.ppermute(gathers[:, lines - halo:], 'xline', [(d, d + 1) for d in ran...  2.39 us
  transfers between devices with their start and end apart: 3, of which 3 were waited for; matrix products, arithmetic and copies ran while one was open for 0% of the time, Pallas kernels for 0%

profile of v1, /device:TPU:0, one launch (start us, length us, event | category | flops | bytes accessed | tf_op | source)
XLA Modules:
  0.0 81.7 jit_solution(17429483185688578987)
XLA Ops:
  6.5 0.0 all-gather.2.cloned.1.call-start
  6.5 0.7 all-gather.2.cloned.1.call-update
  7.3 2.4 %collective-permute-start = (bf16[2,6,96,256]{3,2,1,0:T(8,128)(2,1)}, bf16[2,6,96,256]{3,2,1,0:T(8,128)(2,1)S(1)}, u32[]{:S(2)}, u32[]{:S(2)}) collective-permute-start(bf16[2,6,96,256]{3,2,1,0:T(8,128)(2,1)} %own_ref.1), channel_id=1, source_target_pairs={{0,1},{1,2},{2,3},{3,4},{4,5},{5,6},{6,7},{7,8},{8,9},{9,10},{10,1... | collective-permute-start | bytes 1769480 | tf_op jit(solution)/shard_map/ppermute | solution.py:152
  9.7 1.3 %collective-permute-start.1 = (bf16[2,6,96,256]{3,2,1,0:T(8,128)(2,1)}, bf16[2,6,96,256]{3,2,1,0:T(8,128)(2,1)S(1)}, u32[]{:S(2)}, u32[]{:S(2)}) collective-permute-start(bf16[2,6,96,256]{3,2,1,0:T(8,128)(2,1)} %own_ref.1), channel_id=1, source_target_pairs={{1,0},{2,1},{3,2},{4,3},{5,4},{6,5},{7,6},{8,7},{9,8},{10,9},{11,1... | collective-permute-start | bytes 1769480 | tf_op jit(solution)/shard_map/ppermute | solution.py:155
  11.0 0.5 collective-permute-done.left_ref
  11.4 4.4 %collective-permute-done.1.right_ref = bf16[2,6,96,256]{3,2,1,0:T(8,128)(2,1)S(1)} collective-permute-done((bf16[2,6,96,256]{3,2,1,0:T(8,128)(2,1)}, bf16[2,6,96,256]{3,2,1,0:T(8,128)(2,1)S(1)}, u32[]{:S(2)}, u32[]{:S(2)}) %collective-permute-start.1) | collective-permute-done | bytes 589856 | tf_op jit(solution)/shard_map/ppermute | solution.py:155
  15.9 38.5 %all-gather.2.cloned.1.call-done.radon_ref = bf16[32,2,96,96]{3,2,1,0:T(8,128)(2,1)} async-done(((bf16[2,2,96,96]{3,2,1,0:T(8,128)(2,1)}), bf16[32,2,96,96]{3,2,1,0:T(8,128)(2,1)}) %all-gather.2.cloned.1.call-update) | async-done | bytes 1179664 | tf_op jit(solution)/shard_map/all_gather | solution.py:151
  54.4 0.0 copy-start
  54.4 1.4 %copy-done = bf16[32,2,96,96]{3,2,1,0:T(8,128)(2,1)S(1)} copy-done((bf16[32,2,96,96]{3,2,1,0:T(8,128)(2,1)S(1)}, bf16[32,2,96,96]{3,2,1,0:T(8,128)(2,1)}, u32[]{:S(2)}) %copy-start) | copy-done | bytes 1179672
  55.8 0.0 copy-start.1
  55.8 1.1 %copy-done.1 = bf16[2,6,96,256]{3,2,1,0:T(8,128)(2,1)S(1)} copy-done((bf16[2,6,96,256]{3,2,1,0:T(8,128)(2,1)S(1)}, bf16[2,6,96,256]{3,2,1,0:T(8,128)(2,1)}, u32[]{:S(2)}) %copy-start.1) | copy-done | bytes 589848
  56.9 0.0 copy-start.2
  56.9 0.9 %copy-done.2 = bf16[256,256]{1,0:T(8,128)(2,1)S(1)} copy-done((bf16[256,256]{1,0:T(8,128)(2,1)S(1)}, bf16[256,256]{1,0:T(8,128)(2,1)}, u32[]{:S(2)}) %copy-start.2) | copy-done | bytes 131096
  57.8 0.0 copy-start.3
  57.8 0.9 %copy-done.3 = bf16[256,256]{1,0:T(8,128)(2,1)S(1)} copy-done((bf16[256,256]{1,0:T(8,128)(2,1)S(1)}, bf16[256,256]{1,0:T(8,128)(2,1)}, u32[]{:S(2)}) %copy-start.3) | copy-done | bytes 131096
  58.7 0.0 copy-start.4
  58.7 0.8 copy-done.4
  59.4 0.0 copy-start.5
  59.4 0.8 copy-done.5
  60.2 0.0 copy-start.6
  60.2 0.7 copy-done.6
  60.8 14.0 %shard_map.73 = bf16[2,6,96,256]{3,2,1,0:T(8,128)(2,1)} custom-call(f32[2]{0:T(128)S(1)} %copy-done.6, bf16[2,6,96,256]{3,2,1,0:T(8,128)(2,1)S(1)} %copy-done.1, bf16[2,6,96,256]{3,2,1,0:T(8,128)(2,1)S(1)} %collective-permute-done.left_ref, bf16[2,6,96,256]{3,2,1,0:T(8,128)(2,1)S(1)} %collective-permute-done.1.right_ref, ...), custom_call_target="tpu_custom_call" | custom-call | tf_op jit(solution)/shard_map/pallas_call | solution.py:160
Async XLA Ops:
  6.5 47.9 %all-gather.2.cloned.1.call-start = ((), (), s32[]{:S(2)}) async-start(), calls=%async_computation | async-start | bytes 1671168 | tf_op jit(solution)/shard_map/all_gather | solution.py:151
  7.3 4.2 %collective-permute-start = (bf16[2,6,96,256]{3,2,1,0:T(8,128)(2,1)}, bf16[2,6,96,256]{3,2,1,0:T(8,128)(2,1)S(1)}, u32[]{:S(2)}, u32[]{:S(2)}) collective-permute-start(bf16[2,6,96,256]{3,2,1,0:T(8,128)(2,1)} %own_ref.1), channel_id=1, source_target_pairs={{0,1},{1,2},{2,3},{3,4},{4,5},{5,6},{6,7},{7,8},{8,9},{9,10},{10,1... | collective-permute-start | bytes 1769480 | tf_op jit(solution)/shard_map/ppermute | solution.py:152
  9.7 6.2 %collective-permute-start.1 = (bf16[2,6,96,256]{3,2,1,0:T(8,128)(2,1)}, bf16[2,6,96,256]{3,2,1,0:T(8,128)(2,1)S(1)}, u32[]{:S(2)}, u32[]{:S(2)}) collective-permute-start(bf16[2,6,96,256]{3,2,1,0:T(8,128)(2,1)} %own_ref.1), channel_id=1, source_target_pairs={{1,0},{2,1},{3,2},{4,3},{5,4},{6,5},{7,6},{8,7},{9,8},{10,9},{11,1... | collective-permute-start | bytes 1769480 | tf_op jit(solution)/shard_map/ppermute | solution.py:155
  54.4 1.4 %copy-start = (bf16[32,2,96,96]{3,2,1,0:T(8,128)(2,1)S(1)}, bf16[32,2,96,96]{3,2,1,0:T(8,128)(2,1)}, u32[]{:S(2)}) copy-start(bf16[32,2,96,96]{3,2,1,0:T(8,128)(2,1)} %all-gather.2.cloned.1.call-done.radon_ref) | copy-start | bytes 3538948
  55.8 1.1 %copy-start.1 = (bf16[2,6,96,256]{3,2,1,0:T(8,128)(2,1)S(1)}, bf16[2,6,96,256]{3,2,1,0:T(8,128)(2,1)}, u32[]{:S(2)}) copy-start(bf16[2,6,96,256]{3,2,1,0:T(8,128)(2,1)} %own_ref.1) | copy-start | bytes 1769476
  56.9 0.9 %copy-start.2 = (bf16[256,256]{1,0:T(8,128)(2,1)S(1)}, bf16[256,256]{1,0:T(8,128)(2,1)}, u32[]{:S(2)}) copy-start(bf16[256,256]{1,0:T(8,128)(2,1)} %constant.11.clone.box_ref) | copy-start | bytes 393220
  57.8 0.9 %copy-start.3 = (bf16[256,256]{1,0:T(8,128)(2,1)S(1)}, bf16[256,256]{1,0:T(8,128)(2,1)}, u32[]{:S(2)}) copy-start(bf16[256,256]{1,0:T(8,128)(2,1)} %constant.10.clone.diff_ref) | copy-start | bytes 393220
  58.7 0.8 copy-start.4
  59.4 0.8 copy-start.5
  60.2 0.7 copy-start.6
Sparse Core Ops, SparseCore 0:
  9.6 44.7 all-gather.1

commit v2 on v1

--- a/solution.py
+++ b/solution.py
@@ -10,6 +10,7 @@
 from jax.experimental.pallas import tpu as pltpu
 from jax.sharding import PartitionSpec as P
 
+MESH = pl.DeviceIdType.MESH
 ROWS = 16
 
 
@@ -77,22 +78,128 @@
 
 
 def kernel(
-    tau_ref, own_ref, left_ref, right_ref, radon_ref, forward_ref, inverse_ref, diff_ref, box_ref,
-    out_ref, first_s, field_s, half_s, gz_s, prod_s, tens_s, fx_s, fz_s, smooth_s, spec_s, filt_s,
+    tau_ref, own_hbm, radon_hbm, table_hbm, out_ref,
+    own_ref, left_ref, right_ref, radon_ref, table_ref,
+    first_s, field_s, half_s, gz_s, prod_s, tens_s, fx_s, fz_s, smooth_s, spec_s, filt_s,
+    local_sem, halo_send, halo_recv, radon_send, radon_recv,
 ):
     inlines, lines, offsets, depth = own_ref.shape
     halo = left_ref.shape[1]
     steps = halo // 3
     bins = radon_ref.shape[0]
+    share = radon_hbm.shape[0]
+    devices = bins // share
+    chips = devices // 2
     me = lax.axis_index("xline")
+    chip, core = me // 2, me % 2
+    sibling = chip * 2 + 1 - core
+
+    barrier = pltpu.get_barrier_semaphore()
+
+    def greet(j, carry):
+        pl.semaphore_signal(
+            barrier, inc=1, device_id={"xline": (me + j) % devices}, device_id_type=MESH
+        )
+        return carry
+
+    lax.fori_loop(1, devices, greet, 0)
+
+    block = pl.ds(pl.multiple_of(me * share, share), share)
+    local = [
+        pltpu.make_async_copy(own_hbm, own_ref, local_sem.at[0]),
+        pltpu.make_async_copy(table_hbm, table_ref, local_sem.at[1]),
+        pltpu.make_async_copy(radon_hbm, radon_ref.at[block], local_sem.at[2]),
+    ]
+    for copy in local:
+        copy.start()
+
+    @pl.when(me == 0)
+    def _():
+        left_ref[...] = jnp.zeros_like(left_ref)
+
+    @pl.when(me == devices - 1)
+    def _():
+        right_ref[...] = jnp.zeros_like(right_ref)
+
+    pl.semaphore_wait(barrier, devices - 1)
+
+    def to_right(inline):
+        return pltpu.make_async_remote_copy(
+            src_ref=own_hbm.at[inline, pl.ds(lines - halo, halo)],
+            dst_ref=left_ref.at[inline],
+            send_sem=halo_send.at[0, inline],
+            recv_sem=halo_recv.at[0, inline],
+            device_id={"xline": (me + 1) % devices},
+            device_id_type=MESH,
+        )
+
+    def to_left(inline):
+        return pltpu.make_async_remote_copy(
+            src_ref=own_hbm.at[inline, pl.ds(0, halo)],
+            dst_ref=right_ref.at[inline],
+            send_sem=halo_send.at[1, inline],
+            recv_sem=halo_recv.at[1, inline],
+            device_id={"xline": (me + devices - 1) % devices},
+            device_id_type=MESH,
+        )
+
+    def send_halo(inline):
+        @pl.when(me < devices - 1)
+        def _():
+            to_right(inline).start()
+
+        @pl.when(me > 0)
+        def _():
+            to_left(inline).start()
+
+    def spread(target):
+        return pltpu.make_async_remote_copy(
+            src_ref=radon_hbm,
+            dst_ref=radon_ref.at[block],
+            send_sem=radon_send.at[target],
+            recv_sem=radon_recv.at[me],
+            device_id={"xline": target},
+            device_id_type=MESH,
+        )
+
+    def forward(source):
+        held = radon_ref.at[pl.ds(pl.multiple_of(source * share, share), share)]
+        return pltpu.make_async_remote_copy(
+            src_ref=held,
+            dst_ref=held,
+            send_sem=radon_send.at[source + 1 - 2 * core],
+            recv_sem=radon_recv.at[source],
+            device_id={"xline": sibling},
+            device_id_type=MESH,
+        )
+
+    def same_core(j):
+        return (chip + j) % chips * 2 + core
+
+    def each_chip(action):
+        def body(j, carry):
+            action(same_core(j))
+            return carry
+
+        lax.fori_loop(1, chips, body, 0)
+
+    send_halo(0)
+    each_chip(lambda target: spread(target).start())
+    spread(sibling).start()
+    for inline in range(1, inlines):
+        send_halo(inline)
+    for copy in local:
+        copy.wait()
+
+    diff_ref = table_ref.at[pl.ds(4 * bins, depth)]
+    box_ref = table_ref.at[pl.ds(4 * bins + depth, depth)]
     keep_left = jnp.where(me > 0, 1.0, 0.0).astype(jnp.float32)
-    keep_right = jnp.where(me < lax.axis_size("xline") - 1, 1.0, 0.0).astype(jnp.float32)
+    keep_right = jnp.where(me < devices - 1, 1.0, 0.0).astype(jnp.float32)
     scratch = (field_s, half_s, gz_s, prod_s, tens_s, fx_s, fz_s, diff_ref, box_ref)
     blocks = offsets // ROWS
 
-    def chunk(number, carry):
-        inline = number // blocks
-        at = pl.ds(pl.multiple_of(number % blocks * ROWS, ROWS), ROWS)
+    def chunk(inline, number):
+        at = pl.ds(pl.multiple_of(number * ROWS, ROWS), ROWS)
         for x in range(halo):
             half_s[rows_of(x), :] = left_ref[inline, x, at, :]
             half_s[rows_of(halo + lines + x), :] = right_ref[inline, x, at, :]
@@ -115,15 +222,39 @@
             )
             for x, value in results:
                 smooth_s[inline * lines + x, at, :] = value.astype(jnp.bfloat16)
-        return carry
-
-    lax.fori_loop(0, inlines * blocks, chunk, 0)
+        return inline
+
+    for inline in range(inlines):
+
+        @pl.when(me > 0)
+        def _():
+            to_right(inline).wait_recv()
+
+        @pl.when(me < devices - 1)
+        def _():
+            to_left(inline).wait_recv()
+
+        def one(number, carry):
+            chunk(inline, number)
+            return carry
+
+        lax.fori_loop(0, blocks, one, 0)
+        if inline == 0:
+
+            def pass_on(source):
+                forward(source).wait_recv()
+                forward(source).start()
+
+            each_chip(pass_on)
 
     count = inlines * lines
     slots = spec_s.shape[0] // (2 * bins)
     for n in range(count):
-        value = dot_on(forward_ref[...], smooth_s[n], 1, 1)
+        value = dot_on(table_ref[pl.ds(0, 2 * bins), :], smooth_s[n], 1, 1)
         spec_s[pl.ds(n, 2 * bins, stride=slots), :] = value.astype(jnp.bfloat16).astype(jnp.float32)
+
+    forward(sibling).wait_recv()
+    each_chip(lambda source: forward(source + 1 - 2 * core).wait_recv())
 
     def one_bin(k, carry):
         base = pl.multiple_of(k * 2 * slots, 2 * slots)
@@ -139,8 +270,26 @@
     lax.fori_loop(0, bins, one_bin, 0, unroll=8)
     for n in range(count):
         value = filt_s[pl.ds(n, 2 * bins, stride=slots), :].astype(jnp.bfloat16)
-        result = dot_on(value, inverse_ref[...], 0, 0)
+        result = dot_on(value, table_ref[pl.ds(2 * bins, 2 * bins), :], 0, 0)
         out_ref[n // lines, n % lines] = result.astype(jnp.bfloat16)
+
+    for inline in range(inlines):
+
+        @pl.when(me < devices - 1)
+        def _():
+            to_right(inline).wait_send()
+
+        @pl.when(me > 0)
+        def _():
+            to_left(inline).wait_send()
+
+    spread(sibling).wait_send()
+
+    def finish(peer):
+        spread(peer).wait_send()
+        forward(peer).wait_send()
+
+    each_chip(finish)
 
 
 def per_device(gathers, time_steps, radon_op):
@@ -148,21 +297,22 @@
     devices = lax.axis_size("xline")
     bins = radon_op.shape[0] * devices
     halo = 3 * time_steps.shape[0]
-    operators = lax.all_gather(radon_op, "xline", axis=0, tiled=True)
-    left = lax.ppermute(
-        gathers[:, lines - halo :], "xline", [(d, d + 1) for d in range(devices - 1)]
-    )
-    right = lax.ppermute(gathers[:, :halo], "xline", [(d + 1, d) for d in range(devices - 1)])
     width = lines + 2 * halo
     slots = -(-inlines * lines // 16) * 16
-    vmem = pl.BlockSpec(memory_space=pltpu.VMEM)
+    table = np.concatenate(tables(depth, bins), axis=0)
+    hbm = pl.BlockSpec(memory_space=pl.ANY)
     f32, bf16 = jnp.float32, jnp.bfloat16
     return pl.pallas_call(
         kernel,
         out_shape=jax.ShapeDtypeStruct(gathers.shape, bf16),
-        in_specs=[pl.BlockSpec(memory_space=pltpu.SMEM)] + [vmem] * 8,
-        out_specs=vmem,
+        in_specs=[pl.BlockSpec(memory_space=pltpu.SMEM), hbm, hbm, hbm],
+        out_specs=pl.BlockSpec(memory_space=pltpu.VMEM),
         scratch_shapes=[
+            pltpu.VMEM(gathers.shape, bf16),
+            pltpu.VMEM((inlines, halo, offsets, depth), bf16),
+            pltpu.VMEM((inlines, halo, offsets, depth), bf16),
+            pltpu.VMEM((bins,) + radon_op.shape[1:], bf16),
+            pltpu.VMEM(table.shape, bf16),
             pltpu.VMEM((width * ROWS, depth), f32),
             pltpu.VMEM((width * ROWS, depth), f32),
             pltpu.VMEM((width * ROWS, depth), bf16),
@@ -174,9 +324,16 @@
             pltpu.VMEM((inlines * lines, offsets, depth), bf16),
             pltpu.VMEM((2 * bins * slots, offsets), f32),
             pltpu.VMEM((2 * bins * slots, offsets), f32),
+            pltpu.SemaphoreType.DMA((3,)),
+            pltpu.SemaphoreType.DMA((2, inlines)),
+            pltpu.SemaphoreType.DMA((2, inlines)),
+            pltpu.SemaphoreType.DMA((devices,)),
+            pltpu.SemaphoreType.DMA((devices,)),
         ],
-        compiler_params=pltpu.CompilerParams(vmem_limit_bytes=48 * 2**20),
-    )(time_steps, gathers, left, right, operators, *tables(depth, bins))
+        compiler_params=pltpu.CompilerParams(
+            collective_id=0, has_side_effects=True, vmem_limit_bytes=48 * 2**20
+        ),
+    )(time_steps, gathers, radon_op, table)
 
 
 def solution(mesh):

time: 82.1 us -> 41.8 us (0.51)
  the two profiles are of different devices: /device:TPU:0 before, /device:TPU:13 now
where the time goes in v2:
time: 41.8 us; the launch traced here: 41.6 us
  Pallas kernels  37.2 us (89%)
  local copies, waits for them, and re-layouts  4.4 us (11%)
    pallas_call x1, Pallas kernels, per_device(): pl.pallas_call(kernel, out_shape=jax.ShapeDtypeStruct(gathers.shape, bf16...  37.2 us
    unnamed x9, local copies, waits for them, and re-layouts  4.4 us

profile of v2, /device:TPU:13, one launch (start us, length us, event | category | flops | bytes accessed | tf_op | source)
XLA Modules:
  0.0 41.6 jit_solution(3547011251460423487)
XLA Ops:
  0.0 0.0 copy-start
  0.0 1.1 %copy-done = bf16[2,6,96,256]{3,2,1,0:T(8,128)(2,1)S(1)} copy-done((bf16[2,6,96,256]{3,2,1,0:T(8,128)(2,1)S(1)}, bf16[2,6,96,256]{3,2,1,0:T(8,128)(2,1)}, u32[]{:S(2)}) %copy-start) | copy-done | bytes 589848
  1.1 0.0 copy-start.1
  1.1 1.0 %copy-done.1 = bf16[640,256]{1,0:T(8,128)(2,1)S(1)} copy-done((bf16[640,256]{1,0:T(8,128)(2,1)S(1)}, bf16[640,256]{1,0:T(8,128)(2,1)}, u32[]{:S(2)}) %copy-start.1) | copy-done | bytes 327704
  2.0 0.0 copy-start.2
  2.0 0.9 %copy-done.2 = bf16[2,2,96,96]{3,2,1,0:T(8,128)(2,1)S(1)} copy-done((bf16[2,2,96,96]{3,2,1,0:T(8,128)(2,1)S(1)}, bf16[2,2,96,96]{3,2,1,0:T(8,128)(2,1)}, u32[]{:S(2)}) %copy-start.2) | copy-done | bytes 73752
  2.9 0.0 copy-start.3
  2.9 0.7 %copy-done.3 = f32[2]{0:T(128)S(1)} copy-done((f32[2]{0:T(128)S(1)}, f32[2]{0:T(128)}, u32[]{:S(2)}) %copy-start.3) | copy-done | bytes 32
  3.6 37.2 %shard_map.46 = bf16[2,6,96,256]{3,2,1,0:T(8,128)(2,1)S(1)} custom-call(f32[2]{0:T(128)S(1)} %copy-done.3, bf16[2,6,96,256]{3,2,1,0:T(8,128)(2,1)S(1)} %copy-done, bf16[2,2,96,96]{3,2,1,0:T(8,128)(2,1)S(1)} %copy-done.2, bf16[640,256]{1,0:T(8,128)(2,1)S(1)} %copy-done.1), custom_call_target="tpu_custom_call" | custom-call | tf_op jit(solution)/shard_map/pallas_call | solution.py:305
  40.8 0.8 %copy.6 = bf16[2,6,96,256]{3,2,1,0:T(8,128)(2,1)} copy(bf16[2,6,96,256]{3,2,1,0:T(8,128)(2,1)S(1)} %shard_map.46) | data formatting | bytes 1179648
Async XLA Ops:
  0.0 1.1 %copy-start = (bf16[2,6,96,256]{3,2,1,0:T(8,128)(2,1)S(1)}, bf16[2,6,96,256]{3,2,1,0:T(8,128)(2,1)}, u32[]{:S(2)}) copy-start(bf16[2,6,96,256]{3,2,1,0:T(8,128)(2,1)} %own_hbm.1) | copy-start | bytes 1769476
  1.1 1.0 %copy-start.1 = (bf16[640,256]{1,0:T(8,128)(2,1)S(1)}, bf16[640,256]{1,0:T(8,128)(2,1)}, u32[]{:S(2)}) copy-start(bf16[640,256]{1,0:T(8,128)(2,1)} %constant.2.clone.table_hbm) | copy-start | bytes 983044
  2.0 0.9 %copy-start.2 = (bf16[2,2,96,96]{3,2,1,0:T(8,128)(2,1)S(1)}, bf16[2,2,96,96]{3,2,1,0:T(8,128)(2,1)}, u32[]{:S(2)}) copy-start(bf16[2,2,96,96]{3,2,1,0:T(8,128)(2,1)} %radon_hbm.1) | copy-start | bytes 221188
  2.9 0.7 %copy-start.3 = (f32[2]{0:T(128)S(1)}, f32[2]{0:T(128)}, u32[]{:S(2)}) copy-start(f32[2]{0:T(128)} %tau_ref.1) | copy-start | bytes 28

commit v3 on v2

--- a/solution.py
+++ b/solution.py
@@ -11,7 +11,7 @@
 from jax.sharding import PartitionSpec as P
 
 MESH = pl.DeviceIdType.MESH
-ROWS = 16
+ROWS = 48
 
 
 def tables(depth, bins):
@@ -184,10 +184,10 @@
         lax.fori_loop(1, chips, body, 0)
 
     send_halo(0)
+    for inline in range(1, inlines):
+        send_halo(inline)
     each_chip(lambda target: spread(target).start())
     spread(sibling).start()
-    for inline in range(1, inlines):
-        send_halo(inline)
     for copy in local:
         copy.wait()
 
@@ -239,7 +239,7 @@
             return carry
 
         lax.fori_loop(0, blocks, one, 0)
-        if inline == 0:
+        if inline == inlines - 1:
 
             def pass_on(source):
                 forward(source).wait_recv()
@@ -331,7 +331,7 @@
             pltpu.SemaphoreType.DMA((devices,)),
         ],
         compiler_params=pltpu.CompilerParams(
-            collective_id=0, has_side_effects=True, vmem_limit_bytes=48 * 2**20
+            collective_id=0, has_side_effects=True, vmem_limit_bytes=63 * 2**20
         ),
     )(time_steps, gathers, radon_op, table)
 

time: 41.8 us -> 36.8 us (0.88)
  Pallas kernels: 37.2 us -> 34.7 us
  local copies, waits for them, and re-layouts: 4.4 us -> 1.92 us
    unnamed x9 -> x1, local copies, waits for them, and re-layouts: 4.4 us -> 1.92 us
    pallas_call x1, Pallas kernels: 37.2 us -> 34.7 us  [per_device(): pl.pallas_call(kernel, out_shape=jax.ShapeDtypeStruct(gathers.shape, bf16...]
where the time goes in v3:
time: 36.8 us; the launch traced here: 36.6 us
  Pallas kernels  34.7 us (94%)
  local copies, waits for them, and re-layouts  1.92 us (5%)
    pallas_call x1, Pallas kernels, per_device(): pl.pallas_call(kernel, out_shape=jax.ShapeDtypeStruct(gathers.shape, bf16...  34.7 us
    unnamed x1, local copies, waits for them, and re-layouts  1.92 us

profile of v3, /device:TPU:13, one launch (start us, length us, event | category | flops | bytes accessed | tf_op | source)
XLA Modules:
  0.0 36.6 jit_solution(1587124316294563801)
XLA Ops:
  0.0 34.7 %shard_map.46 = bf16[2,6,96,256]{3,2,1,0:T(8,128)(2,1)} custom-call(f32[2]{0:T(128)} %tau_ref.1, bf16[2,6,96,256]{3,2,1,0:T(8,128)(2,1)} %own_hbm.1, bf16[2,2,96,96]{3,2,1,0:T(8,128)(2,1)} %radon_hbm.1, bf16[640,256]{1,0:T(8,128)(2,1)} %constant.2.clone.table_hbm), custom_call_target="tpu_custom_call" | custom-call | tf_op jit(solution)/shard_map/pallas_call | solution.py:305
  34.7 1.9 %copy.6 = bf16[2,6,96,256]{3,2,1,0:T(8,128)(2,1)} copy(bf16[2,6,96,256]{3,2,1,0:T(8,128)(2,1)} %shard_map.46) | data formatting | bytes 1179648
